TPU v7x, 128 devices: a whole 4x4x4 slice. The times are simulated.
128 devices in a mesh: tm: 8 (over y, core), expert: 16 (over z, x).
Axes of the slice: x: 4, y: 4, z: 4, core: 2. Of those that a mesh axis runs over, the one named last changes fastest.
Arguments:
- queries: bfloat16 [16384, 2048], P(('tm', 'expert')), may hold values from -6 to 6
- keys: bfloat16 [16384, 2048], P(('tm', 'expert')), may hold values from -6 to 6
- values: bfloat16 [16384, 2048], P(('tm', 'expert')), may hold values from -6 to 6
- out_grad: bfloat16 [16384, 2048], P(('tm', 'expert')), may hold values from -6 to 6
- expert_ids: int32 [16384, 2], P(('tm', 'expert')), may hold values from 0 to 31, all different within a row
- combine_gates: float32 [16384, 2], P(('tm', 'expert')), may hold values from 0.2 to 1
- gate_weight: bfloat16 [128, 2048, 512], P(('tm', 'expert')), may hold values from -0.125 to 0.125
- up_weight: bfloat16 [128, 2048, 512], P(('tm', 'expert')), may hold values from -0.125 to 0.125
- down_weight: bfloat16 [128, 512, 2048], P(('tm', 'expert')), may hold values from -0.125 to 0.125
Outputs:
- query_grad: bfloat16 [16384, 2048], P(('tm', 'expert'))
- key_grad: bfloat16 [16384, 2048], P(('tm', 'expert'))
- value_grad: bfloat16 [16384, 2048], P(('tm', 'expert'))
- gate_weight_grad: float32 [128, 2048, 512], P(('tm', 'expert'))
- up_weight_grad: float32 [128, 2048, 512], P(('tm', 'expert'))
- down_weight_grad: float32 [128, 512, 2048], P(('tm', 'expert'))
Inputs may be any that keep to these rules, and one draw needn't show every extreme that they name: `expert_ids`: the two experts of a token differ.
All inputs are finite; a program needn't handle non-finite values.
Results may differ from a plain program's by a relative error of at most 0.017.
Values may be sent and summed in bfloat16 or wider, within the bound.
A program may use at most 192 MiB of HBM per device.

v0:
```python
import jax
import jax.numpy as jnp
from jax import lax
from jax.sharding import PartitionSpec as P

HEADS = 16
HEAD_DIM = 128
SLICES = 4
epsilon = 1e-06
highest = lax.Precision.HIGHEST


def side_by_side(arrays, axis, split_dim, concat_dim, along):
    widths = [a.shape[along] for a in arrays]
    both = jnp.concatenate(arrays, axis=along)
    whole = lax.all_to_all(both, axis, split_axis=split_dim, concat_axis=concat_dim, tiled=True)
    return tuple(jnp.split(whole, [sum(widths[:k]) for k in range(1, len(widths))], axis=along))


def slot_places(routes, capacity, experts):
    flat_ids = routes.reshape(-1)
    onehot = (flat_ids[:, None] == jnp.arange(experts, dtype=jnp.int32)[None, :]).astype(jnp.int32)
    earlier = jnp.cumsum(onehot, axis=0) - onehot
    position = jnp.sum(earlier * onehot, axis=1)
    return jnp.where(position < capacity, flat_ids * capacity + position, experts * capacity)


def expert_slice(rows, grad_rows, gate_part, up_part, down_part):
    gate = jnp.dot(rows, gate_part, preferred_element_type=jnp.float32)
    upper = jnp.dot(rows, up_part, preferred_element_type=jnp.float32)
    sigma = jax.nn.sigmoid(gate)
    act = (gate * sigma * upper).astype(jnp.bfloat16)
    act_grad = jnp.dot(grad_rows, down_part.T, preferred_element_type=jnp.float32)
    down_grad = jnp.dot(act.T, grad_rows, preferred_element_type=jnp.float32)
    gate_grad = (act_grad * upper * sigma * (1.0 + gate * (1.0 - sigma))).astype(jnp.bfloat16)
    up_grad = (act_grad * gate * sigma).astype(jnp.bfloat16)
    gate_wgrad = jnp.dot(rows.T, gate_grad, preferred_element_type=jnp.float32)
    up_wgrad = jnp.dot(rows.T, up_grad, preferred_element_type=jnp.float32)
    partial_sum = jnp.dot(gate_grad, gate_part.T, preferred_element_type=jnp.float32)
    partial_sum = partial_sum + jnp.dot(up_grad, up_part.T, preferred_element_type=jnp.float32)
    return (partial_sum.astype(jnp.bfloat16), gate_wgrad, up_wgrad, down_grad)


def body(
    queries, keys, values, out_grad, expert_ids, combine_gates, gate_weight, up_weight, down_weight
):
    tok_rows = queries.shape[0]
    width = queries.shape[1]
    time_count = lax.axis_size("tm")
    group_count = lax.axis_size("expert")
    devices = time_count * group_count
    experts = devices // SLICES
    capacity = SLICES * max(1, 3 * tok_rows // (experts * SLICES))
    shape3 = (tok_rows, HEADS, HEAD_DIM)
    query_f = queries.astype(jnp.float32).reshape(shape3)
    key_f = keys.astype(jnp.float32).reshape(shape3)
    value_f = values.astype(jnp.float32).reshape(shape3)
    local = jnp.einsum("tha,thb->hab", key_f, value_f, precision=highest)
    everyone = lax.all_gather(local[None], "tm", axis=0, tiled=True)
    mine = lax.axis_index("tm")
    picks = (jnp.arange(everyone.shape[0], dtype=jnp.int32) <= mine).astype(jnp.float32)
    inclusive = jnp.einsum("c,chab->hab", picks, everyone, precision=highest)
    states = lax.psum(inclusive, "expert")
    mixed = jnp.einsum("tha,hab->thb", query_f, states, precision=highest)
    scale = lax.rsqrt(jnp.mean(mixed * mixed, axis=-1, keepdims=True) + epsilon)
    normed = mixed * scale
    hidden = normed.astype(jnp.bfloat16).reshape(tok_rows, width)
    places = slot_places(expert_ids, capacity, experts)
    rows_h = jnp.repeat(hidden, 2, axis=0)
    grad_f = out_grad.astype(jnp.float32)
    rows_g = (jnp.repeat(grad_f, 2, axis=0) * combine_gates.reshape(-1, 1)).astype(jnp.bfloat16)
    buffer_h = (
        jnp.zeros((experts * capacity, width), jnp.bfloat16).at[places].set(rows_h, mode="drop")
    )
    buffer_g = (
        jnp.zeros((experts * capacity, width), jnp.bfloat16).at[places].set(rows_g, mode="drop")
    )
    send_h = jnp.repeat(buffer_h.reshape(experts, capacity, width), SLICES, axis=0)
    send_g = jnp.repeat(buffer_g.reshape(experts, capacity, width), SLICES, axis=0)
    got_h, got_g = side_by_side((send_h, send_g), ("tm", "expert"), 0, 0, 1)
    got_h = got_h.reshape(1, devices, capacity, width)
    got_g = got_g.reshape(1, devices, capacity, width)
    rows = got_h.reshape(-1, width)
    grad_rows = got_g.reshape(-1, width)
    partial_sum, gate_wgrad, up_wgrad, down_grad = expert_slice(
        rows, grad_rows, gate_weight[0], up_weight[0], down_weight[0]
    )
    payload = partial_sum.astype(jnp.float32).reshape(devices, capacity, width)
    returned = lax.all_to_all(
        payload.astype(jnp.bfloat16), ("tm", "expert"), split_axis=0, concat_axis=0, tiled=True
    ).astype(payload.dtype)
    summed = jnp.sum(returned.reshape(experts, SLICES, capacity, width), axis=1)
    per_choice = jnp.take(
        summed.reshape(experts * capacity, width), places, axis=0, mode="fill", fill_value=0.0
    )
    moe_grad = jnp.sum(per_choice.reshape(tok_rows, 2, width), axis=1)
    hidden_grad = (grad_f + moe_grad).reshape(shape3)
    norm_grad = scale * (
        hidden_grad - normed * jnp.mean(hidden_grad * normed, axis=-1, keepdims=True)
    )
    query_grad = jnp.einsum("thb,hab->tha", norm_grad, states, precision=highest)
    local_back = jnp.einsum("tha,thb->hab", query_f, norm_grad, precision=highest)
    every_back = lax.all_gather(
        local_back[None].astype(jnp.bfloat16), "tm", axis=0, tiled=True
    ).astype(jnp.float32)
    mine_back = lax.axis_index("tm")
    picks_back = (jnp.arange(every_back.shape[0], dtype=jnp.int32) >= mine_back).astype(jnp.float32)
    inclusive_back = jnp.einsum("c,chab->hab", picks_back, every_back, precision=highest)
    back_states = lax.psum(inclusive_back.astype(jnp.bfloat16), "expert").astype(jnp.float32)
    key_grad = jnp.einsum("thb,hab->tha", value_f, back_states, precision=highest)
    value_grad = jnp.einsum("tha,hab->thb", key_f, back_states, precision=highest)
    return (
        query_grad.reshape(tok_rows, width).astype(jnp.bfloat16),
        key_grad.reshape(tok_rows, width).astype(jnp.bfloat16),
        value_grad.reshape(tok_rows, width).astype(jnp.bfloat16),
        gate_wgrad[None],
        up_wgrad[None],
        down_grad[None],
    )


def solution(mesh):
    placed = (
        P(("tm", "expert"), None),
        P(("tm", "expert"), None),
        P(("tm", "expert"), None),
        P(("tm", "expert"), None),
        P(("tm", "expert"), None),
        P(("tm", "expert"), None),
        P(("tm", "expert"), None, None),
        P(("tm", "expert"), None, None),
        P(("tm", "expert"), None, None),
    )
    return jax.shard_map(
        body,
        mesh=mesh,
        in_specs=placed,
        out_specs=(
            P(("tm", "expert"), None),
            P(("tm", "expert"), None),
            P(("tm", "expert"), None),
            P(("tm", "expert"), None, None),
            P(("tm", "expert"), None, None),
            P(("tm", "expert"), None, None),
        ),
        check_vma=False,
    )
```

profile of v0, /device:TPU:0, one launch (start us, length us, event | category | flops | bytes accessed | tf_op | source)
XLA Modules:
  0.0 693.4 jit_solution(2359564202389222377)
XLA Ops:
  10.0 52.6 %all-gather.5.cloned.1.call-done = f32[128,128,128]{2,1,0:T(8,128)} async-done(((f32[16,128,128]{2,1,0:T(8,128)}), f32[128,128,128]{2,1,0:T(8,128)}) %all-gather.5.cloned.1.call-update) | async-done | bytes 8388624 | tf_op jit(solution)/shard_map/all_gather | solution.py:59
  62.5 11.8 %fusion = f32[1,16,128,128]{3,0,2,1:T(1,128)S(1)} fusion(f32[8,16,128,128]{3,2,1,0:T(8,128)} %bitcast.136, s32[]{:T(128)S(6)} %axis_index.19), kind=kOutput, calls=%fused_computation.6 | convolution fusion | flops 25165832 | bytes 9437188 | tf_op jit(solution)/shard_map/c,chab->hab/dot_general | solution.py:62
  85.4 4.5 scatter_custom_fusion.1
  93.5 70.4 %all-reduce.3.cloned.1.call-done = f32[16,128,128]{1,2,0:T(8,128)} async-done(((f32[16,128,128]{1,2,0:T(8,128)}), f32[16,128,128]{1,2,0:T(8,128)}) %all-reduce.3.cloned.1.call-update) | async-done | bytes 1048592 | tf_op jit(solution)/shard_map/psum | solution.py:63
  179.2 6.1 broadcast_in_dim.53
  189.5 9.2 %pad_maximum_fusion = bf16[128,24,2048]{2,1,0:T(8,128)(2,1)S(1)} fusion(bf16[128,12,2048]{2,1,0:T(8,128)(2,1)} %bitcast.132, bf16[128,12,2048]{2,1,0:T(8,128)(2,1)} %bitcast.133), kind=kLoop, calls=%fused_computation.4 | loop fusion | flops 25165824 | bytes 25165824 | tf_op jit(solution)/shard_map/concatenate | solution.py:15
  198.7 149.2 %all_to_all.10 = bf16[128,24,2048]{2,1,0:T(8,128)(2,1)S(1)} all-to-all(bf16[128,24,2048]{2,1,0:T(8,128)(2,1)S(1)} %pad_maximum_fusion), channel_id=1, replica_groups=mesh['tm'=8,'expert'=16] {'tm','expert'}, dimensions={0} | all-to-all | bytes 25165824 | tf_op jit(solution)/shard_map/all_to_all | solution.py:16
  347.9 7.1 %fusion.46 = (bf16[128,12,2048]{2,1,0:T(8,128)(2,1)}, bf16[128,12,2048]{2,1,0:T(8,128)(2,1)}) fusion(bf16[128,24,2048]{2,1,0:T(8,128)(2,1)S(1)} %all_to_all.10), kind=kLoop, calls=%fused_computation.84 | loop fusion | bytes 25165824 | tf_op jit(solution)/shard_map/split | solution.py:17
  355.0 10.7 %reshape_reshape.6 = bf16[1536,2048]{1,0:T(8,128)(2,1)} reshape(bf16[128,12,2048]{2,1,0:T(8,128)(2,1)} %get-tuple-element.24) | data formatting | bytes 12582912 | tf_op jit(solution)/shard_map/reshape;reshape | solution.py:84
  365.7 10.7 %reshape_reshape.7 = bf16[1536,2048]{1,0:T(8,128)(2,1)} reshape(bf16[128,12,2048]{2,1,0:T(8,128)(2,1)} %get-tuple-element.25) | data formatting | bytes 12582912 | tf_op jit(solution)/shard_map/reshape;reshape | solution.py:83
  376.4 6.0 fusion.6
  385.9 4.8 multiply_convert_fusion.1
  390.8 6.5 fusion.4
  397.3 8.5 %add_convert_fusion = bf16[1536,2048]{1,0:T(8,128)(2,1)} fusion(f32[1536,2048]{1,0:T(8,128)} %fusion.4, bf16[1536,512]{1,0:T(8,128)(2,1)S(1)} %get-tuple-element.26, bf16[1,2048,512]{2,1,0:T(8,128)(2,1)S(1)} %copy-done.13), kind=kOutput, calls=%fused_computation.5 | convolution fusion | flops 3227516928 | bytes 22544384 | tf_op jit(solution)/shard_map/dot_general | solution.py:40
  405.8 10.6 %convert_element_type.88 = bf16[128,12,2048]{2,1,0:T(8,128)(2,1)} reshape(bf16[1536,2048]{1,0:T(8,128)(2,1)} %add_convert_fusion) | data formatting | bytes 12582912 | tf_op jit(solution)/shard_map/convert_element_type | solution.py:90
  416.4 6.9 all-to-all-start.1
  423.6 99.8 %all-to-all-done.1 = bf16[128,12,2048]{2,1,0:T(8,128)(2,1)} async-done(((bf16[128,12,2048]{2,1,0:T(8,128)(2,1)}), bf16[128,12,2048]{2,1,0:T(8,128)(2,1)}, u32[]{:S(2)}, u32[]{:S(2)}) %all-to-all-start.1) | async-done | bytes 6291488 | tf_op jit(solution)/shard_map/all_to_all | solution.py:89
  523.4 7.8 %convert_reduce_fusion = f32[32,12,2048]{2,1,0:T(8,128)} fusion(bf16[128,12,2048]{2,1,0:T(8,128)(2,1)} %all-to-all-done.1), kind=kLoop, calls=%fused_computation.3 | loop fusion | flops 5505024 | bytes 9437184 | tf_op jit(solution)/shard_map/reduce_sum | solution.py:92
  548.2 8.9 %convolution_bitcast_fusion.1 = f32[1,2048,512]{2,1,0:T(8,128)} fusion(bf16[1536,2048]{1,0:T(8,128)(2,1)} %reshape_reshape.7, bf16[1536,512]{1,0:T(8,128)(2,1)} %copy-done.14), kind=kOutput, calls=%fused_computation.11 | convolution fusion | flops 3221225472 | bytes 12058624 | tf_op jit(solution)/shard_map/dot_general | solution.py:38
  557.1 8.3 %convolution_bitcast_fusion = f32[1,512,2048]{2,1,0:T(8,128)} fusion(bf16[1536,2048]{1,0:T(8,128)(2,1)} %reshape_reshape.6, f32[1536,512]{1,0:T(8,128)S(1)} %copy-done.19, f32[1536,512]{1,0:T(8,128)S(1)} %copy-done.17), kind=kOutput, calls=%fused_computation.10 | convolution fusion | flops 3225944064 | bytes 16777216 | tf_op jit(solution)/shard_map/dot_general | solution.py:34
  565.4 24.5 %all-gather.7.cloned.1.call-done = bf16[128,128,128]{2,1,0:T(8,128)(2,1)} async-done(((bf16[16,128,128]{2,1,0:T(8,128)(2,1)}), bf16[128,128,128]{2,1,0:T(8,128)(2,1)}) %all-gather.7.cloned.1.call-update) | async-done | bytes 4194320 | tf_op jit(solution)/shard_map/all_gather | solution.py:103
  589.9 4.9 fusion.2
  595.8 8.8 %convolution_bitcast_fusion.2 = f32[1,2048,512]{2,1,0:T(8,128)} fusion(bf16[1536,2048]{1,0:T(8,128)(2,1)} %reshape_reshape.7, bf16[1536,512]{1,0:T(8,128)(2,1)} %copy-done.15), kind=kOutput, calls=%fused_computation.12 | convolution fusion | flops 3221225472 | bytes 12058624 | tf_op jit(solution)/shard_map/dot_general | solution.py:37
  607.6 73.6 %all-reduce.5.cloned.1.call-done = bf16[16,128,128]{2,1,0:T(8,128)(2,1)} async-done(((bf16[16,128,128]{2,1,0:T(8,128)(2,1)}), bf16[16,128,128]{2,1,0:T(8,128)(2,1)}) %all-reduce.5.cloned.1.call-update) | async-done | bytes 524304 | tf_op jit(solution)/shard_map/psum | solution.py:109
  (102 shorter events, 66.5 us)
Async XLA Ops:
  7.2 369.2 %copy-start = (bf16[1,2048,512]{2,1,0:T(8,128)(2,1)S(1)}, bf16[1,2048,512]{2,1,0:T(8,128)(2,1)}, u32[]{:S(2)}) copy-start(bf16[1,2048,512]{2,1,0:T(8,128)(2,1)} %param.15) | copy-start | bytes 6291460
  7.2 55.4 %all-gather.5.cloned.1.call-start = ((), (), s32[]{:S(2)}) async-start(), calls=%async_computation.4 | async-start | bytes 9437184 | tf_op jit(solution)/shard_map/all_gather | solution.py:59
  9.9 154.0 %all-reduce.3.cloned.1.call-start = ((), (), s32[]{:S(2)}) async-start(), calls=%async_computation.2 | async-start | bytes 2097152 | tf_op jit(solution)/shard_map/psum | solution.py:63
  74.4 3.5 copy-start.11
  85.4 78.6 %copy-start.8 = (bf16[128,2048]{1,0:T(8,128)(2,1)S(1)}, bf16[128,2048]{1,0:T(8,128)(2,1)}, u32[]{:S(2)}) copy-start(bf16[128,2048]{1,0:T(8,128)(2,1)} %param.9) | copy-start | bytes 1572868
  179.2 6.1 copy-start.4
  376.4 6.0 copy-start.5
  376.4 6.0 copy-start.13
  376.4 9.5 %slice-start = ((s8[6291456]{0:T(1024)(128)(4,1)}), s8[4194304]{0:T(1024)(128)(4,1)S(1)}, s32[]{:S(2)}) async-start(s8[6291456]{0:T(1024)(128)(4,1)} %bitcast.137), calls=%async_computation.6 | async-start | bytes 8388608
  382.4 3.5 copy-start.16
  382.4 3.5 slice-start.1
  382.4 3.5 copy-start.12
  385.9 4.9 copy-start.18
  390.8 6.5 copy-start.15
  390.8 6.5 copy-start.14
  416.4 106.9 %all-to-all-start.1 = ((bf16[128,12,2048]{2,1,0:T(8,128)(2,1)}), bf16[128,12,2048]{2,1,0:T(8,128)(2,1)}, u32[]{:S(2)}, u32[]{:S(2)}) async-start(bf16[128,12,2048]{2,1,0:T(8,128)(2,1)} %convert_element_type.88), calls=%async_computation.1 | async-start | bytes 16777216 | tf_op jit(solution)/shard_map/all_to_all | solution.py:89
  423.3 166.6 %all-gather.7.cloned.1.call-start = ((), (), s32[]{:S(2)}) async-start(), calls=%async_computation.5 | async-start | bytes 4718592 | tf_op jit(solution)/shard_map/all_gather | solution.py:103
  539.4 4.5 copy-start.7
  548.2 133.0 %all-reduce.5.cloned.1.call-start = ((), (), s32[]{:S(2)}) async-start(), calls=%async_computation.3 | async-start | bytes 1048576 | tf_op jit(solution)/shard_map/psum | solution.py:109
  548.2 8.9 %copy-start.17 = (f32[1536,512]{1,0:T(8,128)S(1)}, f32[1536,512]{1,0:T(8,128)}, u32[]{:S(2)}) copy-start(f32[1536,512]{1,0:T(8,128)} %copy-done.16) | copy-start | bytes 9437188
  548.2 8.9 %copy-start.19 = (f32[1536,512]{1,0:T(8,128)S(1)}, f32[1536,512]{1,0:T(8,128)}, u32[]{:S(2)}) copy-start(f32[1536,512]{1,0:T(8,128)} %copy-done.18) | copy-start | bytes 9437188
  595.8 8.8 %copy-start.6 = (f32[16,128,128]{1,2,0:T(8,128)S(1)}, f32[16,128,128]{1,2,0:T(8,128)}, u32[]{:S(2)}) copy-start(f32[16,128,128]{1,2,0:T(8,128)} %all-reduce.3.cloned.1.call-done) | copy-start | bytes 3145732
  604.6 76.6 %copy-start.9 = (bf16[128,2048]{1,0:T(8,128)(2,1)S(1)}, bf16[128,2048]{1,0:T(8,128)(2,1)}, u32[]{:S(2)}) copy-start(bf16[128,2048]{1,0:T(8,128)(2,1)} %param.11) | copy-start | bytes 1572868
  606.6 79.9 %copy-start.1 = (bf16[1,2048,512]{2,1,0:T(8,128)(2,1)S(1)}, bf16[1,2048,512]{2,1,0:T(8,128)(2,1)}, u32[]{:S(2)}) copy-start(bf16[1,2048,512]{2,1,0:T(8,128)(2,1)} %param.15) | copy-start | bytes 6291460
  (3 other events, 4.4 us)
Sparse Core Ops, SparseCore 0:
  10.3 52.1 all-gather.4
  76.7 87.2 all-reduce.2
  548.3 41.5 all-gather.6
  595.9 85.2 all-reduce.4
where the time goes:
time: 702 us; the launch traced here: 693 us
  waiting for transfers between devices  321 us (46%)
  blocking collectives  149 us (21%)
  local copies, waits for them, and re-layouts  89.3 us (13%)
  matrix products  84.1 us (12%)
  other arithmetic  28.2 us (4%)
  between operations  14.6 us (2%)
    all_to_all x1, blocking collectives, side_by_side(): lax.all_to_all(both, axis, split_axis=split_dim, concat_axis=concat_dim,...  149 us
    all_to_all x1, waiting for transfers between devices, body(): lax.all_to_all(payload.astype(jnp.bfloat16), ('tm', 'expert'), split_axis...  99.8 us
    psum x1, waiting for transfers between devices, body(): lax.psum(inclusive_back.astype(jnp.bfloat16), 'expert').astype(jnp.float32)  73.6 us
    psum x1, waiting for transfers between devices, body(): states = lax.psum(inclusive, 'expert')  70.4 us
    all_gather x1, waiting for transfers between devices, body(): everyone = lax.all_gather(local[None], 'tm', axis=0, tiled=True)  52.6 us
    all_gather x1, waiting for transfers between devices, body(): lax.all_gather(local_back[None].astype(jnp.bfloat16), 'tm', axis=0, tiled...  24.5 us
  transfers between devices with their start and end apart: 5, of which 5 were waited for; matrix products, arithmetic and copies ran while one was open for 7% of the time, Pallas kernels for 0%

commit v1 on v0

--- a/solution.py
+++ b/solution.py
@@ -56,7 +56,9 @@
     key_f = keys.astype(jnp.float32).reshape(shape3)
     value_f = values.astype(jnp.float32).reshape(shape3)
     local = jnp.einsum("tha,thb->hab", key_f, value_f, precision=highest)
-    everyone = lax.all_gather(local[None], "tm", axis=0, tiled=True)
+    everyone = jnp.concatenate(
+        lax.all_to_all(jnp.stack([local[None]] * lax.axis_size("tm")), "tm", 0, 0), axis=0
+    )
     mine = lax.axis_index("tm")
     picks = (jnp.arange(everyone.shape[0], dtype=jnp.int32) <= mine).astype(jnp.float32)
     inclusive = jnp.einsum("c,chab->hab", picks, everyone, precision=highest)

time: 702 us -> 754 us (1.074)
  waiting for transfers between devices: 321 us -> 363 us
    all_to_all x0 -> x1, waiting for transfers between devices: none -> 94.6 us  [body(): lax.all_to_all(jnp.stack([local[None]] * lax.axis_size('tm')), 'tm', 0, 0)]
    all_gather x1 -> x0, waiting for transfers between devices: 52.6 us -> none  [body(): everyone = lax.all_gather(local[None], 'tm', axis=0, tiled=True)]
  transfers between devices with their start and end apart: 5 -> 5, of which waited for: 5 -> 5; matrix products, arithmetic and copies ran while one was open for 7% -> 6% of each run, Pallas kernels for 0% -> 0%
where the time goes in v1:
time: 754 us; the launch traced here: 745 us
  waiting for transfers between devices  363 us (48%)
  blocking collectives  149 us (20%)
  local copies, waits for them, and re-layouts  94.7 us (13%)
  matrix products  83.1 us (11%)
  other arithmetic  28.2 us (4%)
  between operations  14.5 us (2%)
  starting transfers between devices  11.9 us (2%)
    all_to_all x1, blocking collectives, side_by_side(): lax.all_to_all(both, axis, split_axis=split_dim, concat_axis=concat_dim,...  149 us
    all_to_all x1, waiting for transfers between devices, body(): lax.all_to_all(payload.astype(jnp.bfloat16), ('tm', 'expert'), split_axis...  99.8 us
    all_to_all x1, waiting for transfers between devices, body(): lax.all_to_all(jnp.stack([local[None]] * lax.axis_size('tm')), 'tm', 0, 0)  94.6 us
    psum x1, waiting for transfers between devices, body(): lax.psum(inclusive_back.astype(jnp.bfloat16), 'expert').astype(jnp.float32)  73.6 us
    psum x1, waiting for transfers between devices, body(): states = lax.psum(inclusive, 'expert')  70.7 us
    all_gather x1, waiting for transfers between devices, body(): lax.all_gather(local_back[None].astype(jnp.bfloat16), 'tm', axis=0, tiled...  24.5 us
  transfers between devices with their start and end apart: 5, of which 5 were waited for; matrix products, arithmetic and copies ran while one was open for 6% of the time, Pallas kernels for 0%

profile of v1, /device:TPU:0, one launch (start us, length us, event | category | flops | bytes accessed | tf_op | source)
XLA Modules:
  0.0 744.9 jit_solution(14245292321587091811)
XLA Ops:
  13.2 4.9 all-to-all-start
  18.2 94.6 %all-to-all-done = f32[8,1,16,128,128]{4,3,2,1,0:T(8,128)} async-done(((f32[8,1,16,128,128]{4,3,2,1,0:T(8,128)}), f32[8,1,16,128,128]{4,3,2,1,0:T(8,128)}, u32[]{:S(2)}, u32[]{:S(2)}) %all-to-all-start) | async-done | bytes 8388640 | tf_op jit(solution)/shard_map/all_to_all | solution.py:60
  112.7 11.8 %fusion = f32[1,16,128,128]{3,0,2,1:T(1,128)S(1)} fusion(f32[8,16,128,128]{3,2,1,0:T(8,128)} %bitcast.2, s32[]{:T(128)S(6)} %axis_index.19), kind=kOutput, calls=%fused_computation.6 | convolution fusion | flops 25165832 | bytes 9437188 | tf_op jit(solution)/shard_map/c,chab->hab/dot_general | solution.py:64
  143.7 70.7 %all-reduce.3.cloned.1.call-done = f32[16,128,128]{1,2,0:T(8,128)} async-done(((f32[16,128,128]{1,2,0:T(8,128)}), f32[16,128,128]{1,2,0:T(8,128)}) %all-reduce.3.cloned.1.call-update) | async-done | bytes 1048592 | tf_op jit(solution)/shard_map/psum | solution.py:65
  229.6 6.1 broadcast_in_dim.49
  240.0 9.2 %pad_maximum_fusion = bf16[128,24,2048]{2,1,0:T(8,128)(2,1)S(1)} fusion(bf16[128,12,2048]{2,1,0:T(8,128)(2,1)} %bitcast.132, bf16[128,12,2048]{2,1,0:T(8,128)(2,1)} %bitcast.133), kind=kLoop, calls=%fused_computation.4 | loop fusion | flops 25165824 | bytes 25165824 | tf_op jit(solution)/shard_map/concatenate | solution.py:15
  249.2 149.1 %all_to_all.15 = bf16[128,24,2048]{2,1,0:T(8,128)(2,1)S(1)} all-to-all(bf16[128,24,2048]{2,1,0:T(8,128)(2,1)S(1)} %pad_maximum_fusion), channel_id=1, replica_groups=mesh['tm'=8,'expert'=16] {'tm','expert'}, dimensions={0} | all-to-all | bytes 25165824 | tf_op jit(solution)/shard_map/all_to_all | solution.py:16
  398.3 7.1 fusion.46
  405.5 10.7 %reshape_reshape.6 = bf16[1536,2048]{1,0:T(8,128)(2,1)} reshape(bf16[128,12,2048]{2,1,0:T(8,128)(2,1)} %get-tuple-element.24) | data formatting | bytes 12582912 | tf_op jit(solution)/shard_map/reshape;reshape | solution.py:86
  416.2 10.7 %reshape_reshape.7 = bf16[1536,2048]{1,0:T(8,128)(2,1)} reshape(bf16[128,12,2048]{2,1,0:T(8,128)(2,1)} %get-tuple-element.25) | data formatting | bytes 12582912 | tf_op jit(solution)/shard_map/reshape;reshape | solution.py:85
  426.9 6.0 fusion.6
  437.4 4.8 multiply_convert_fusion.1
  442.3 6.5 fusion.4
  448.8 8.5 %add_convert_fusion = bf16[1536,2048]{1,0:T(8,128)(2,1)} fusion(f32[1536,2048]{1,0:T(8,128)} %fusion.4, bf16[1536,512]{1,0:T(8,128)(2,1)S(1)} %get-tuple-element.26, bf16[1,2048,512]{2,1,0:T(8,128)(2,1)S(1)} %copy-done.14), kind=kOutput, calls=%fused_computation.5 | convolution fusion | flops 3227516928 | bytes 22544384 | tf_op jit(solution)/shard_map/dot_general | solution.py:40
  457.3 10.6 %convert_element_type.88 = bf16[128,12,2048]{2,1,0:T(8,128)(2,1)} reshape(bf16[1536,2048]{1,0:T(8,128)(2,1)} %add_convert_fusion) | data formatting | bytes 12582912 | tf_op jit(solution)/shard_map/convert_element_type | solution.py:92
  467.9 6.9 all-to-all-start.2
  475.1 99.8 %all-to-all-done.2 = bf16[128,12,2048]{2,1,0:T(8,128)(2,1)} async-done(((bf16[128,12,2048]{2,1,0:T(8,128)(2,1)}), bf16[128,12,2048]{2,1,0:T(8,128)(2,1)}, u32[]{:S(2)}, u32[]{:S(2)}) %all-to-all-start.2) | async-done | bytes 6291488 | tf_op jit(solution)/shard_map/all_to_all | solution.py:91
  574.9 7.8 %convert_reduce_fusion = f32[32,12,2048]{2,1,0:T(8,128)} fusion(bf16[128,12,2048]{2,1,0:T(8,128)(2,1)} %all-to-all-done.2), kind=kLoop, calls=%fused_computation.3 | loop fusion | flops 5505024 | bytes 9437184 | tf_op jit(solution)/shard_map/reduce_sum | solution.py:94
  599.7 8.9 %convolution_bitcast_fusion.1 = f32[1,2048,512]{2,1,0:T(8,128)} fusion(bf16[1536,2048]{1,0:T(8,128)(2,1)} %reshape_reshape.7, bf16[1536,512]{1,0:T(8,128)(2,1)} %copy-done.15), kind=kOutput, calls=%fused_computation.11 | convolution fusion | flops 3221225472 | bytes 12058624 | tf_op jit(solution)/shard_map/dot_general | solution.py:38
  608.6 8.3 %convolution_bitcast_fusion = f32[1,512,2048]{2,1,0:T(8,128)} fusion(bf16[1536,2048]{1,0:T(8,128)(2,1)} %reshape_reshape.6, f32[1536,512]{1,0:T(8,128)S(1)} %copy-done.20, f32[1536,512]{1,0:T(8,128)S(1)} %copy-done.18), kind=kOutput, calls=%fused_computation.10 | convolution fusion | flops 3225944064 | bytes 16777216 | tf_op jit(solution)/shard_map/dot_general | solution.py:34
  616.9 24.5 %all-gather.3.cloned.1.call-done = bf16[128,128,128]{2,1,0:T(8,128)(2,1)} async-done(((bf16[16,128,128]{2,1,0:T(8,128)(2,1)}), bf16[128,128,128]{2,1,0:T(8,128)(2,1)}) %all-gather.3.cloned.1.call-update) | async-done | bytes 4194320 | tf_op jit(solution)/shard_map/all_gather | solution.py:105
  641.4 4.9 fusion.2
  647.3 8.8 %convolution_bitcast_fusion.2 = f32[1,2048,512]{2,1,0:T(8,128)} fusion(bf16[1536,2048]{1,0:T(8,128)(2,1)} %reshape_reshape.7, bf16[1536,512]{1,0:T(8,128)(2,1)} %copy-done.16), kind=kOutput, calls=%fused_computation.12 | convolution fusion | flops 3221225472 | bytes 12058624 | tf_op jit(solution)/shard_map/dot_general | solution.py:37
  659.1 73.6 %all-reduce.5.cloned.1.call-done = bf16[16,128,128]{2,1,0:T(8,128)(2,1)} async-done(((bf16[16,128,128]{2,1,0:T(8,128)(2,1)}), bf16[16,128,128]{2,1,0:T(8,128)(2,1)}) %all-reduce.5.cloned.1.call-update) | async-done | bytes 524304 | tf_op jit(solution)/shard_map/psum | solution.py:111
  (99 shorter events, 75.3 us)
Async XLA Ops:
  7.2 419.7 %copy-start = (bf16[1,2048,512]{2,1,0:T(8,128)(2,1)S(1)}, bf16[1,2048,512]{2,1,0:T(8,128)(2,1)}, u32[]{:S(2)}) copy-start(bf16[1,2048,512]{2,1,0:T(8,128)(2,1)} %param.15) | copy-start | bytes 6291460
  13.2 99.6 %all-to-all-start = ((f32[8,1,16,128,128]{4,3,2,1,0:T(8,128)}), f32[8,1,16,128,128]{4,3,2,1,0:T(8,128)}, u32[]{:S(2)}, u32[]{:S(2)}) async-start(f32[8,1,16,128,128]{4,3,2,1,0:T(8,128)} %stack.3), calls=%async_computation | async-start | bytes 16777216 | tf_op jit(solution)/shard_map/all_to_all | solution.py:60
  18.1 196.3 %all-reduce.3.cloned.1.call-start = ((), (), s32[]{:S(2)}) async-start(), calls=%async_computation.3 | async-start | bytes 2097152 | tf_op jit(solution)/shard_map/psum | solution.py:65
  124.6 2.1 copy-start.11
  124.6 3.5 copy-start.12
  135.5 78.9 %copy-start.9 = (bf16[128,2048]{1,0:T(8,128)(2,1)S(1)}, bf16[128,2048]{1,0:T(8,128)(2,1)}, u32[]{:S(2)}) copy-start(bf16[128,2048]{1,0:T(8,128)(2,1)} %param.9) | copy-start | bytes 1572868
  229.6 6.1 copy-start.4
  426.8 6.0 copy-start.5
  426.8 6.0 copy-start.14
  432.9 3.5 copy-start.17
  432.9 3.9 copy-start.6
  432.9 4.5 copy-start.13
  437.4 4.8 copy-start.19
  442.3 6.6 copy-start.16
  442.3 6.5 copy-start.15
  467.9 106.9 %all-to-all-start.2 = ((bf16[128,12,2048]{2,1,0:T(8,128)(2,1)}), bf16[128,12,2048]{2,1,0:T(8,128)(2,1)}, u32[]{:S(2)}, u32[]{:S(2)}) async-start(bf16[128,12,2048]{2,1,0:T(8,128)(2,1)} %convert_element_type.88), calls=%async_computation.2 | async-start | bytes 16777216 | tf_op jit(solution)/shard_map/all_to_all | solution.py:91
  474.8 166.6 %all-gather.3.cloned.1.call-start = ((), (), s32[]{:S(2)}) async-start(), calls=%async_computation.5 | async-start | bytes 4718592 | tf_op jit(solution)/shard_map/all_gather | solution.py:105
  590.9 4.5 copy-start.8
  599.7 133.0 %all-reduce.5.cloned.1.call-start = ((), (), s32[]{:S(2)}) async-start(), calls=%async_computation.4 | async-start | bytes 1048576 | tf_op jit(solution)/shard_map/psum | solution.py:111
  599.7 8.9 %copy-start.18 = (f32[1536,512]{1,0:T(8,128)S(1)}, f32[1536,512]{1,0:T(8,128)}, u32[]{:S(2)}) copy-start(f32[1536,512]{1,0:T(8,128)} %copy-done.17) | copy-start | bytes 9437188
  599.7 8.9 %copy-start.20 = (f32[1536,512]{1,0:T(8,128)S(1)}, f32[1536,512]{1,0:T(8,128)}, u32[]{:S(2)}) copy-start(f32[1536,512]{1,0:T(8,128)} %copy-done.19) | copy-start | bytes 9437188
  647.3 8.8 %copy-start.7 = (f32[16,128,128]{1,2,0:T(8,128)S(1)}, f32[16,128,128]{1,2,0:T(8,128)}, u32[]{:S(2)}) copy-start(f32[16,128,128]{1,2,0:T(8,128)} %all-reduce.3.cloned.1.call-done) | copy-start | bytes 3145732
  656.1 76.6 %copy-start.10 = (bf16[128,2048]{1,0:T(8,128)(2,1)S(1)}, bf16[128,2048]{1,0:T(8,128)(2,1)}, u32[]{:S(2)}) copy-start(bf16[128,2048]{1,0:T(8,128)(2,1)} %param.11) | copy-start | bytes 1572868
  658.1 79.9 %copy-start.1 = (bf16[1,2048,512]{2,1,0:T(8,128)(2,1)S(1)}, bf16[1,2048,512]{2,1,0:T(8,128)(2,1)}, u32[]{:S(2)}) copy-start(bf16[1,2048,512]{2,1,0:T(8,128)(2,1)} %param.15) | copy-start | bytes 6291460
  (2 other events, 2.3 us)
Sparse Core Ops, SparseCore 0:
  126.8 87.5 all-reduce.2
  599.8 41.5 all-gather.2
  647.4 85.2 all-reduce.4
